TPU v7x, 512 devices: a whole 4x8x8 slice. The times are simulated.
512 devices in a mesh: dp: 8 (over y_hi, core), fsdp: 64 (over x, z, y_lo).
Axes of the slice: x: 4, y: 8 (y_hi: 4, y_lo: 2; y = y_hi * 2 + y_lo), z: 8, core: 2. Of those that a mesh axis runs over, the one named last changes fastest.
Arguments:
- tokens: bfloat16 [65536, 4096], P(('dp', 'fsdp')), may hold values from -6 to 6
- out_grad: bfloat16 [65536, 14336], P(('dp', 'fsdp')), may hold values from -0.01171875 to 0.01171875
- basis: bfloat16 [4096, 64], P('fsdp'), may hold values from -0.75 to 0.75
- first_moment: float32 [64, 14336], P('dp', 'fsdp'), may hold values from -0.6 to 0.6
- second_moment: float32 [64, 14336], P('dp', 'fsdp'), may hold values from 0.0005 to 0.002
Outputs:
- update: bfloat16 [4096, 14336], P('fsdp', 'dp')
- new_first: float32 [64, 14336], P('dp', 'fsdp')
- new_second: float32 [64, 14336], P('dp', 'fsdp')
All inputs are finite; a program needn't handle non-finite values.
Results may differ from a plain program's by a relative error of at most 0.0048.
Values may be sent and summed in bfloat16 or wider, within the bound.
A program may use at most 64 MiB of HBM per device.

v0:
```python
import jax
import jax.numpy as jnp
from jax import lax
from jax.sharding import PartitionSpec as P

beta_one = 0.9
beta_two = 0.999
corr_one = 1.0 - 0.9**10
corr_two = 1.0 - 0.999**10
adam_eps = 1e-08
step_rate = 4.0


def per_device(tokens, out_grad, basis, first_moment, second_moment):
    n_replica = lax.axis_size("dp")
    rank = basis.shape[1]
    width = out_grad.shape[1]
    whole_basis = lax.all_gather(basis, "fsdp", axis=0, tiled=True)
    coords = jnp.dot(tokens, whole_basis, preferred_element_type=jnp.float32).astype(jnp.bfloat16)
    rank_part = rank // n_replica
    local_grad = lax.dot_general(
        coords, out_grad, (((0,), (0,)), ((), ())), preferred_element_type=jnp.float32
    )
    summed = lax.psum(local_grad, "dp")
    owned = lax.psum_scatter(summed, "fsdp", scatter_dimension=1, tiled=True)
    grad = lax.dynamic_slice_in_dim(owned, lax.axis_index("dp") * rank_part, rank_part, 0)
    new_first = beta_one * first_moment + (1.0 - beta_one) * grad
    new_second = beta_two * second_moment + (1.0 - beta_two) * grad * grad
    step = new_first / corr_one / (jnp.sqrt(new_second / corr_two) + adam_eps)
    span = width // n_replica
    step_full_rank = lax.all_gather(step, "dp", axis=0, tiled=True)
    step_whole = lax.all_gather(step_full_rank, "fsdp", axis=1, tiled=True)
    step_mine = lax.dynamic_slice_in_dim(step_whole, lax.axis_index("dp") * span, span, 1)
    update = -step_rate * jnp.dot(
        basis.astype(jnp.float32), step_mine, precision=lax.Precision.HIGHEST
    )
    return (update.astype(jnp.bfloat16), new_first, new_second)


def solution(mesh):
    placed = (
        P(("dp", "fsdp"), None),
        P(("dp", "fsdp"), None),
        P("fsdp", None),
        P("dp", "fsdp"),
        P("dp", "fsdp"),
    )
    return jax.shard_map(
        per_device,
        mesh=mesh,
        in_specs=placed,
        out_specs=(P("fsdp", "dp"), P("dp", "fsdp"), P("dp", "fsdp")),
        check_vma=False,
    )
```

profile of v0, /device:TPU:16, one launch (start us, length us, event | category | flops | bytes accessed | tf_op | source)
XLA Modules:
  0.0 892.3 jit_solution(14343511786075393424)
XLA Ops:
  7.2 0.0 copy-start
  7.2 0.0 reduce-scatter.4.cloned.1.call-start
  7.2 171.3 %all_gather.9 = bf16[4096,64]{1,0:T(8,128)(2,1)S(1)} all-gather(bf16[64,64]{1,0:T(8,128)(2,1)} %param.7), channel_id=1, replica_groups=mesh['dp'=8,'fsdp'=64] {'fsdp'}, dimensions={0}, use_global_device_ids=true | all-gather | bytes 532480 | tf_op jit(solution)/shard_map/all_gather | solution.py:18
  178.5 0.0 copy-done
  178.5 7.1 convolution_bitcast_fusion
  185.6 0.0 copy-start.2
  185.6 0.0 copy-start.3
  185.6 0.0 reduce-scatter.4.cloned.1.call-update
  185.7 0.0 all-gather.3.cloned.1.call-start
  185.7 334.7 %reduce-scatter.4.cloned.1.call-done = f32[224,64]{1,0:T(8,128)} async-done(((f32[14336,64]{1,0:T(8,128)}), f32[224,64]{1,0:T(8,128)}) %reduce-scatter.4.cloned.1.call-update) | async-done | bytes 57360
  520.4 1.0 copy.11
  521.4 26.2 %psum.8 = f32[64,224]{1,0:T(8,128)S(1)} all-reduce(f32[64,224]{1,0:T(8,128)S(1)} %copy.11), channel_id=1, replica_groups=mesh['dp'=8,'fsdp'=64] {'dp'}, use_global_device_ids=true, to_apply=%region_0.0 | all-reduce | flops 14336 | bytes 114688 | tf_op jit(solution)/shard_map/psum | solution.py:24
  547.7 0.0 copy-done.2
  547.7 0.0 copy-done.3
  547.7 0.6 add_divide_fusion
  548.3 15.9 %all_gather.10 = f32[64,224]{1,0:T(8,128)} all-gather(f32[8,224]{1,0:T(8,128)S(1)} %get-tuple-element.3), channel_id=1, replica_groups=mesh['dp'=8,'fsdp'=64] {'dp'}, dimensions={0}, use_global_device_ids=true | all-gather | bytes 64512 | tf_op jit(solution)/shard_map/all_gather | solution.py:31
  564.2 0.0 all-gather.3.cloned.1.call-update
  564.2 306.9 %all-gather.3.cloned.1.call-done = f32[64,224,64]{1,2,0:T(8,128)} async-done(((f32[1,224,64]{1,2,0:T(8,128)}), f32[64,224,64]{1,2,0:T(8,128)}) %all-gather.3.cloned.1.call-update) | async-done | bytes 3670032 | tf_op jit(solution)/shard_map/all_gather | solution.py:32
  871.1 6.6 copy.9
  877.7 0.0 copy-start.1
  877.7 5.7 reshape.7
  883.4 0.0 copy-done.1
  883.4 2.1 fusion.1
Async XLA Ops:
  7.2 171.4 %copy-start = (bf16[128,4096]{1,0:T(8,128)(2,1)S(1)}, bf16[128,4096]{1,0:T(8,128)(2,1)}, u32[]{:S(2)}) copy-start(bf16[128,4096]{1,0:T(8,128)(2,1)} %param.5) | copy-start | bytes 3145732
  7.2 513.3 %reduce-scatter.4.cloned.1.call-start = ((), (), s32[]{:S(2)}) async-start(), calls=%async_computation.2 | async-start | bytes 7454720
  185.6 362.0 %copy-start.2 = (f32[8,224]{1,0:T(8,128)S(1)}, f32[8,224]{1,0:T(8,128)}, u32[]{:S(2)}) copy-start(f32[8,224]{1,0:T(8,128)} %param.8) | copy-start | bytes 21508
  185.6 362.0 %copy-start.3 = (f32[8,224]{1,0:T(8,128)S(1)}, f32[8,224]{1,0:T(8,128)}, u32[]{:S(2)}) copy-start(f32[8,224]{1,0:T(8,128)} %param.9) | copy-start | bytes 21508
  185.7 685.4 %all-gather.3.cloned.1.call-start = ((), (), s32[]{:S(2)}) async-start(), calls=%async_computation.1 | async-start | bytes 4259840 | tf_op jit(solution)/shard_map/all_gather | solution.py:32
  877.7 5.7 copy-start.1
Sparse Core Ops, SparseCore 0:
  185.8 334.6 reduce-scatter.3
  564.3 306.7 all-gather.2
where the time goes:
time: 893 us; the launch traced here: 892 us
  waiting for transfers between devices  642 us (72%)
  blocking collectives  213 us (24%)
  between operations  14.1 us (2%)
  local copies, waits for them, and re-layouts  13.3 us (1%)
  matrix products  9.15 us (1%)
    unnamed x3, waiting for transfers between devices  335 us
    all_gather x1, waiting for transfers between devices, per_device(): step_whole = lax.all_gather(step_full_rank, 'fsdp', axis=1, tiled=True)  307 us
    all_gather x1, blocking collectives, per_device(): whole_basis = lax.all_gather(basis, 'fsdp', axis=0, tiled=True)  171 us
    psum x1, blocking collectives, per_device(): summed = lax.psum(local_grad, 'dp')  26.2 us
  transfers between devices with their start and end apart: 2, of which 2 were waited for; matrix products, arithmetic and copies ran while one was open for 0% of the time, Pallas kernels for 0%

commit v1 on v0

v1 whole, which is shorter than its diff:
```python
import jax
import jax.numpy as jnp
from jax import lax
from jax.experimental import pallas as pl
from jax.experimental.pallas import tpu as pltpu
from jax.sharding import PartitionSpec as P

beta_one = 0.9
beta_two = 0.999
corr_one = 1.0 - 0.9**10
corr_two = 1.0 - 0.999**10
adam_eps = 1e-08
step_rate = 4.0

F32, BF16 = jnp.float32, jnp.bfloat16
NX, NY, NZ = 4, 8, 8
TOK = 128
D = 4096
RANK = 64
SPAN = 1792
UNIT = 224
WIN = 512
STARTS = (0, 3, 7, 10)


def kernel(
    tok_in, og_in, basis_in, first_in, second_in,
    upd_out, first_out, second_out,
    tok, og, bag, cot, g, xr, zs, zr, ys, yr, sag, mom, new,
    ld_sem, core_send, core_recv, og_recv, ag_send, ag_recv, cot_send, cot_recv,
    x_send, x_recv, z_send, z_recv, y_send, y_recv, mom_send, mom_recv, new_send, new_recv,
):
    d = lax.axis_index("dp")
    f = lax.axis_index("fsdp")
    h, c = d // 2, d % 2
    x, z, p = f // 16, (f // 2) % 8, f % 2
    y = 2 * h + p
    oc = 1 - c

    def dev(x_, y_, z_, c_):
        return ((y_ // 2) * 2 + c_, (x_ * 8 + z_) * 2 + y_ % 2)

    swap = dev(h, 2 * x + p, 4 * c + z % 4, z // 4)
    alone = jnp.logical_and(x == h, z // 4 == c)
    apart = jnp.logical_not(alone)
    other = dev(x, y, z, oc)
    zp = [dev(x, 2 * h + (p + o % 2) % 2, (z + o // 2) % 8, c) for o in range(16)]
    xs = [dev((x + o) % 4, y, z, c) for o in range(4)]

    def remote(src, dst, send, recv, target):
        return pltpu.make_async_remote_copy(
            src_ref=src, dst_ref=dst, send_sem=send, recv_sem=recv,
            device_id=target, device_id_type=pl.DeviceIdType.MESH,
        )

    def await_bytes(ref, sem):
        pltpu.make_async_copy(ref, ref, sem).wait()

    mine = pl.ds(pl.multiple_of(c * TOK, TOK), TOK)
    pltpu.make_async_copy(tok_in, tok.at[mine], ld_sem.at[0]).start()
    for q in range(4):
        cols = pl.ds(pl.multiple_of((2 * q + c) * SPAN, 128), SPAN)
        pltpu.make_async_copy(og_in.at[:, cols], og.at[q, mine], ld_sem.at[1]).start()

    barrier = pltpu.get_barrier_semaphore()

    def greet(target):
        pl.semaphore_signal(barrier, inc=1, device_id=target, device_id_type=pl.DeviceIdType.MESH)

    for o in range(1, 16):
        greet(zp[o])
    for o in range(1, 4):
        greet(xs[o])
    for a in range(1, 4):
        for r in range(2):
            greet(dev(x, 2 * ((h + a) % 4) + r, z, c))
    greet(other)

    @pl.when(apart)
    def _():
        greet(swap)

    bt = jnp.transpose(basis_in[...].astype(F32))
    pieces = [bt[16 * i : 16 * i + 16] for i in range(4)]
    low = jnp.where(c == 0, pieces[0], pieces[2])
    high = jnp.where(c == 0, pieces[1], pieces[3])
    bag[x, 2 * z + p] = jnp.concatenate([low, high], axis=1).astype(BF16)

    pl.semaphore_wait(barrier, jnp.where(alone, 25, 26))

    def gather_start(buf, k):
        slot = buf.at[x, 2 * z + p]
        for o in range(1, 16):
            remote(slot, slot, ag_send.at[k, 0], ag_recv.at[k, 0], zp[o]).start()

    def gather_finish(buf, k):
        await_bytes(buf.at[0, pl.ds(0, 15)], ag_recv.at[k, 0])
        for o in range(1, 4):
            remote(buf.at[x], buf.at[x], ag_send.at[k, 1], ag_recv.at[k, 1], xs[o]).start()
        await_bytes(buf.at[pl.ds(0, 3)], ag_recv.at[k, 1])

    gather_start(bag, 0)
    remote(tok_in, tok.at[mine], core_send.at[0], core_recv.at[0], other).start()
    for q in range(4):
        cols = pl.ds(pl.multiple_of((2 * q + oc) * SPAN, 128), SPAN)
        remote(og_in.at[:, cols], og.at[q, mine], core_send.at[1], og_recv.at[q], other).start()

    @pl.when(apart)
    def _():
        remote(first_in, mom.at[0], mom_send.at[0], mom_recv.at[0], swap).start()
        remote(second_in, mom.at[1], mom_send.at[1], mom_recv.at[1], swap).start()

    @pl.when(alone)
    def _():
        mom[0] = first_in[...]
        mom[1] = second_in[...]

    gather_finish(bag, 0)
    await_bytes(tok.at[mine], ld_sem.at[0])
    await_bytes(tok.at[mine], core_recv.at[0])

    lane = lax.broadcasted_iota(jnp.int32, (16, 128), 1)
    tops, bottoms = [], []
    for k in range(32):
        even = bag[k // 8, 2 * (k % 8)].astype(F32)
        odd = bag[k // 8, 2 * (k % 8) + 1].astype(F32)
        tops.append(jnp.where(lane < 64, even, pltpu.roll(odd, 64, axis=1)).astype(BF16))
        bottoms.append(jnp.where(lane < 64, pltpu.roll(even, 64, axis=1), odd).astype(BF16))
    basis_t = jnp.concatenate(
        [jnp.concatenate(tops, axis=1), jnp.concatenate(bottoms, axis=1)], axis=0
    )
    half = lax.dot_general(
        basis_t, tok[...], (((1,), (1,)), ((), ())), preferred_element_type=F32
    )
    cot[c] = half.astype(BF16)
    remote(cot.at[c], cot.at[c], cot_send, cot_recv, other).start()
    await_bytes(cot.at[c], cot_recv)
    coords_t = cot[...].reshape(RANK, 2 * TOK)

    await_bytes(og.at[:, mine], ld_sem.at[1])
    for q in range(4):
        await_bytes(og.at[q, mine], og_recv.at[q])
        part = jnp.dot(coords_t, og[q], preferred_element_type=F32).astype(BF16)
        for i in range(4):
            g[q, i] = part[16 * i : 16 * i + 16]
        for o in (2, 1, 3):
            remote(
                g.at[q, (x + o) % 4], xr.at[q, o - 1], x_send.at[q], x_recv.at[q], xs[o]
            ).start()

    for pair in range(2):
        sums = []
        for q in (2 * pair, 2 * pair + 1):
            await_bytes(xr.at[q], x_recv.at[q])
            total = g[q, x].astype(F32)
            for o in range(3):
                total = total + xr[q, o].astype(F32)
            sums.append(total)
        for to in range(8):
            s, start = to // 4, 128 * STARTS[to % 4]
            zs[pair, to] = jnp.concatenate(
                [t[8 * s : 8 * s + 8, start : start + WIN] for t in sums], axis=0
            ).astype(BF16)
        for o in (4, 3, 5, 2, 6, 1, 7):
            to = (z + o) % 8
            remote(
                zs.at[pair, to], zr.at[pair, o - 1], z_send.at[pair], z_recv.at[pair],
                dev(x, y, to, c),
            ).start()

    for pair in range(2):
        await_bytes(zr.at[pair], z_recv.at[pair])
        total = zs[pair, z].astype(F32)
        for o in range(7):
            total = total + zr[pair, o].astype(F32)
        for j in range(2):
            for r in range(2):
                to = 2 * (2 * pair + j) + r
                ys[to] = total[8 * j : 8 * j + 8, 128 * r : 128 * r + 384]
    for o in (4, 3, 5, 2, 6, 1, 7):
        to = (y + o) % 8
        remote(ys.at[to], yr.at[o - 1], y_send, y_recv, dev(x, to, z, c)).start()

    row = lax.broadcasted_iota(jnp.int32, (RANK, 128), 0)
    col = lax.broadcasted_iota(jnp.int32, (RANK, 128), 1)
    spread = []
    for s in range(2):
        hit = col == (row // 8) * 16 + row % 8 + 8 * s
        spread.append(jnp.where(hit, -step_rate, 0.0).astype(BF16))
    left = jnp.concatenate(
        [
            jnp.dot(basis_in[...], e, preferred_element_type=F32).astype(BF16)
            for e in spread
        ],
        axis=0,
    )

    @pl.when(apart)
    def _():
        await_bytes(mom.at[0], mom_recv.at[0])
        await_bytes(mom.at[1], mom_recv.at[1])

    await_bytes(yr, y_recv)
    total = ys[y]
    for o in range(7):
        total = total + yr[o]
    shift = (z % 2) * 64 + p * 96
    grad = pltpu.roll(total, 384 - shift, axis=1)[:, :UNIT]
    new_first = beta_one * mom[0] + (1.0 - beta_one) * grad
    new_second = beta_two * mom[1] + (1.0 - beta_two) * grad * grad
    step = new_first / corr_one / (jnp.sqrt(new_second / corr_two) + adam_eps)
    step = jnp.concatenate([step, jnp.zeros((8, 256 - UNIT), F32)], axis=1)
    step = pltpu.roll(step, (96 * (2 * z + p)) % 128, axis=1)
    sag[x, 2 * z + p] = jnp.concatenate([step[:, :128], step[:, 128:]], axis=0).astype(BF16)
    gather_start(sag, 1)
    new[0] = new_first
    new[1] = new_second

    @pl.when(apart)
    def _():
        remote(new.at[0], first_out, new_send.at[0], new_recv.at[0], swap).start()
        remote(new.at[1], second_out, new_send.at[1], new_recv.at[1], swap).start()

    @pl.when(alone)
    def _():
        first_out[...] = new[0]
        second_out[...] = new[1]

    gather_finish(sag, 1)

    lane = lax.broadcasted_iota(jnp.int32, (RANK, 128), 1)
    right = jnp.concatenate(
        [
            jnp.concatenate([sag[i // 2, 8 * (i % 2) + j] for i in range(8)], axis=0)
            for j in range(8)
        ],
        axis=1,
    )
    both = jnp.dot(left, right, preferred_element_type=F32)
    low = [both[:RANK, 128 * j : 128 * j + 128] for j in range(8)]
    high = [both[RANK:, 128 * j : 128 * j + 128] for j in range(8)]
    for b in range(2):
        l, u = low[4 * b : 4 * b + 4], high[4 * b : 4 * b + 4]
        tiles = [
            l[0],
            jnp.where(lane < 96, u[0], l[1]),
            u[1],
            jnp.where(lane < 64, l[1], l[2]),
            u[2],
            jnp.where(lane < 32, l[2], l[3]),
            u[3],
        ]
        for t, tile in enumerate(tiles):
            upd_out[:, 128 * (7 * b + t) : 128 * (7 * b + t) + 128] = tile.astype(BF16)

    for k, buf in ((0, bag), (1, sag)):
        await_bytes(buf.at[0, pl.ds(0, 15)], ag_send.at[k, 0])
        await_bytes(buf.at[pl.ds(0, 3)], ag_send.at[k, 1])
    await_bytes(tok.at[mine], core_send.at[0])
    await_bytes(og.at[:, mine], core_send.at[1])
    await_bytes(cot.at[c], cot_send)
    for q in range(4):
        await_bytes(xr.at[q], x_send.at[q])
    for pair in range(2):
        await_bytes(zr.at[pair], z_send.at[pair])
    await_bytes(yr, y_send)

    @pl.when(apart)
    def _():
        for i, out in enumerate((first_out, second_out)):
            await_bytes(mom.at[i], mom_send.at[i])
            await_bytes(new.at[i], new_send.at[i])
            await_bytes(out, new_recv.at[i])


def per_device(tokens, out_grad, basis, first_moment, second_moment):
    vmem = pl.BlockSpec(memory_space=pltpu.VMEM)
    anywhere = pl.BlockSpec(memory_space=pl.ANY)
    dma = pltpu.SemaphoreType.DMA
    return pl.pallas_call(
        kernel,
        out_shape=(
            jax.ShapeDtypeStruct((RANK, SPAN), BF16),
            jax.ShapeDtypeStruct((8, UNIT), F32),
            jax.ShapeDtypeStruct((8, UNIT), F32),
        ),
        in_specs=[anywhere, anywhere, vmem, vmem, vmem],
        out_specs=[vmem, vmem, vmem],
        scratch_shapes=[
            pltpu.VMEM((2 * TOK, D), BF16),
            pltpu.VMEM((4, 2 * TOK, SPAN), BF16),
            pltpu.VMEM((NX, 16, 16, 128), BF16),
            pltpu.VMEM((2, RANK // 2, 2 * TOK), BF16),
            pltpu.VMEM((4, NX, 16, SPAN), BF16),
            pltpu.VMEM((4, NX - 1, 16, SPAN), BF16),
            pltpu.VMEM((2, NZ, 16, WIN), BF16),
            pltpu.VMEM((2, NZ - 1, 16, WIN), BF16),
            pltpu.VMEM((NY, 8, 384), F32),
            pltpu.VMEM((NY - 1, 8, 384), F32),
            pltpu.VMEM((NX, 16, 16, 128), BF16),
            pltpu.VMEM((2, 8, UNIT), F32),
            pltpu.VMEM((2, 8, UNIT), F32),
            dma((2,)),
            dma((2,)), dma((1,)), dma((4,)),
            dma((2, 2)), dma((2, 2)),
            dma, dma,
            dma((4,)), dma((4,)),
            dma((2,)), dma((2,)),
            dma, dma,
            dma((2,)), dma((2,)),
            dma((2,)), dma((2,)),
        ],
        compiler_params=pltpu.CompilerParams(
            collective_id=0, has_side_effects=True, vmem_limit_bytes=48 << 20
        ),
    )(tokens, out_grad, basis, first_moment, second_moment)


def solution(mesh):
    placed = (
        P(("dp", "fsdp"), None),
        P(("dp", "fsdp"), None),
        P("fsdp", None),
        P("dp", "fsdp"),
        P("dp", "fsdp"),
    )
    return jax.shard_map(
        per_device,
        mesh=mesh,
        in_specs=placed,
        out_specs=(P("fsdp", "dp"), P("dp", "fsdp"), P("dp", "fsdp")),
        check_vma=False,
    )
```

time: 893 us -> 68.5 us (0.08)
  the two profiles are of different devices: /device:TPU:16 before, /device:TPU:8 now
where the time goes in v1:
time: 68.5 us; the launch traced here: 68.2 us
  Pallas kernels  60.3 us (88%)
  local copies, waits for them, and re-layouts  7.25 us (11%)
    pallas_call x1, Pallas kernels, per_device(): pl.pallas_call(kernel, out_shape=(jax.ShapeDtypeStruct((RANK, SPAN), BF16...  60.3 us
    unnamed x13, local copies, waits for them, and re-layouts  7.25 us

profile of v1, /device:TPU:8, one launch (start us, length us, event | category | flops | bytes accessed | tf_op | source)
XLA Modules:
  0.0 68.2 jit_solution(5300019030570291078)
XLA Ops:
  0.6 0.0 copy-start
  0.6 2.0 %copy-done = bf16[128,14336]{1,0:T(8,128)(2,1)S(1)} copy-done((bf16[128,14336]{1,0:T(8,128)(2,1)S(1)}, bf16[128,14336]{1,0:T(8,128)(2,1)}, u32[]{:S(2)}) %copy-start) | copy-done | bytes 3670040
  2.7 0.0 copy-start.1
  2.7 1.2 %copy-done.1 = bf16[128,4096]{1,0:T(8,128)(2,1)S(1)} copy-done((bf16[128,4096]{1,0:T(8,128)(2,1)S(1)}, bf16[128,4096]{1,0:T(8,128)(2,1)}, u32[]{:S(2)}) %copy-start.1) | copy-done | bytes 1048600
  3.9 0.0 copy-start.2
  3.9 0.7 %copy-done.2 = bf16[64,64]{1,0:T(8,128)(2,1)S(1)} copy-done((bf16[64,64]{1,0:T(8,128)(2,1)S(1)}, bf16[64,64]{1,0:T(8,128)(2,1)}, u32[]{:S(2)}) %copy-start.2) | copy-done | bytes 8216
  4.6 0.0 copy-start.3
  4.6 0.7 %copy-done.3 = f32[8,224]{1,0:T(8,128)S(1)} copy-done((f32[8,224]{1,0:T(8,128)S(1)}, f32[8,224]{1,0:T(8,128)}, u32[]{:S(2)}) %copy-start.3) | copy-done | bytes 7192
  5.3 0.0 copy-start.4
  5.3 0.7 %copy-done.4 = f32[8,224]{1,0:T(8,128)S(1)} copy-done((f32[8,224]{1,0:T(8,128)S(1)}, f32[8,224]{1,0:T(8,128)}, u32[]{:S(2)}) %copy-start.4) | copy-done | bytes 7192
  6.0 60.3 %shard_map.76 = (bf16[64,1792]{1,0:T(8,128)(2,1)S(1)}, f32[8,224]{1,0:T(8,128)S(1)}, f32[8,224]{1,0:T(8,128)S(1)}) custom-call(bf16[128,4096]{1,0:T(8,128)(2,1)S(1)} %copy-done.1, bf16[128,14336]{1,0:T(8,128)(2,1)S(1)} %copy-done, bf16[64,64]{1,0:T(8,128)(2,1)S(1)} %copy-done.2, f32[8,224]{1,0:T(8,128)S(1)} %copy-done.3, f32[8,224]{1,0:T(8,128)S(1)} %copy-done.4), custom_call_target="tpu_custom_call" | custom-call | tf_op jit(solution)/shard_map/pallas_call | solution.py:280
  66.3 0.7 %copy.11 = bf16[64,1792]{1,0:T(8,128)(2,1)} copy(bf16[64,1792]{1,0:T(8,128)(2,1)S(1)} %get-tuple-element.6) | data formatting | bytes 458752
  67.0 0.6 copy.12
  67.6 0.6 copy.13
Async XLA Ops:
  0.6 2.0 %copy-start = (bf16[128,14336]{1,0:T(8,128)(2,1)S(1)}, bf16[128,14336]{1,0:T(8,128)(2,1)}, u32[]{:S(2)}) copy-start(bf16[128,14336]{1,0:T(8,128)(2,1)} %og_in.1) | copy-start | bytes 11010052
  2.7 1.2 %copy-start.1 = (bf16[128,4096]{1,0:T(8,128)(2,1)S(1)}, bf16[128,4096]{1,0:T(8,128)(2,1)}, u32[]{:S(2)}) copy-start(bf16[128,4096]{1,0:T(8,128)(2,1)} %tok_in.1) | copy-start | bytes 3145732
  3.9 0.7 %copy-start.2 = (bf16[64,64]{1,0:T(8,128)(2,1)S(1)}, bf16[64,64]{1,0:T(8,128)(2,1)}, u32[]{:S(2)}) copy-start(bf16[64,64]{1,0:T(8,128)(2,1)} %basis_in.1) | copy-start | bytes 24580
  4.6 0.7 %copy-start.3 = (f32[8,224]{1,0:T(8,128)S(1)}, f32[8,224]{1,0:T(8,128)}, u32[]{:S(2)}) copy-start(f32[8,224]{1,0:T(8,128)} %first_in.1) | copy-start | bytes 21508
  5.3 0.7 %copy-start.4 = (f32[8,224]{1,0:T(8,128)S(1)}, f32[8,224]{1,0:T(8,128)}, u32[]{:S(2)}) copy-start(f32[8,224]{1,0:T(8,128)} %second_in.1) | copy-start | bytes 21508

commit v2 on v0

v2 whole, which is shorter than its diff:
```python
import jax
import jax.numpy as jnp
from jax import lax
from jax.experimental import pallas as pl
from jax.experimental.pallas import tpu as pltpu
from jax.sharding import PartitionSpec as P

beta_one = 0.9
beta_two = 0.999
corr_one = 1.0 - 0.9**10
corr_two = 1.0 - 0.999**10
adam_eps = 1e-08
step_rate = 4.0

F32, BF16 = jnp.float32, jnp.bfloat16
NX, NY, NZ = 4, 8, 8
TOK = 128
D = 4096
RANK = 64
SPAN = 1792
UNIT = 224
WIN = 512
STARTS = (0, 3, 7, 10)
FAR = (4, 3, 5, 2, 6, 1, 7)


def await_bytes(ref, sem):
    pltpu.make_async_copy(ref, ref, sem).wait()


def kernel(
    tok_in, og_in, basis_in, first_in, second_in,
    sag, new_out,
    bas, tok, og, bag, cot, g, xr, zs, zr, zs2, zr2, zs3, zr3, xs3, xr3, ys, yr, tile, mom, new,
    ld_sem, core_send, core_recv, og_recv, ag_send, ag_recv, fw_send, fw_recv, cot_send, cot_recv,
    x_send, x_recv, z_send, z_recv, y_send, y_recv, mom_send, mom_recv, new_send, new_recv,
    st_send, st_recv, st_own, ready,
):
    d = lax.axis_index("dp")
    f = lax.axis_index("fsdp")
    h, c = d // 2, d % 2
    x, z, p = f // 16, (f // 2) % 8, f % 2
    y = 2 * h + p
    oc = 1 - c

    def dev(x_, y_, z_, c_):
        return ((y_ // 2) * 2 + c_, (x_ * 8 + z_) * 2 + y_ % 2)

    swap = dev(h, 2 * x + p, 4 * c + z % 4, z // 4)
    alone = jnp.logical_and(x == h, z // 4 == c)
    apart = jnp.logical_not(alone)
    other = dev(x, y, z, oc)
    xs = [dev((x + o) % 4, y, z, c) for o in range(4)]

    def plane(a, b, s):
        return dev((x + a) % 4, 2 * h + (p + s) % 2, (z + b) % 8, c)

    def remote(src, dst, send, recv, target):
        return pltpu.make_async_remote_copy(
            src_ref=src, dst_ref=dst, send_sem=send, recv_sem=recv,
            device_id=target, device_id_type=pl.DeviceIdType.MESH,
        )

    def signal(sem, target):
        pl.semaphore_signal(sem, inc=1, device_id=target, device_id_type=pl.DeviceIdType.MESH)

    barrier = pltpu.get_barrier_semaphore()
    pltpu.make_async_copy(basis_in, bas, ld_sem.at[2]).start()
    for b in FAR + (0,):
        for s in (1, 0):
            if (b, s) != (0, 0):
                signal(barrier, plane(0, b, s))
    for a in (2, 1, 3):
        for r in range(2):
            signal(barrier, dev(x, 2 * ((h + a) % 4) + r, z, c))
    for o in (2, 1, 3):
        signal(barrier, xs[o])
    signal(barrier, other)

    mine = pl.ds(pl.multiple_of(c * TOK, TOK), TOK)
    pltpu.make_async_copy(tok_in, tok.at[mine], ld_sem.at[0]).start()
    for q in range(4):
        cols = pl.ds(pl.multiple_of((2 * q + c) * SPAN, 128), SPAN)
        pltpu.make_async_copy(og_in.at[:, cols], og.at[q, mine], ld_sem.at[1]).start()

    await_bytes(bas, ld_sem.at[2])
    bt = jnp.transpose(bas[...].astype(F32))
    pieces = [bt[16 * i : 16 * i + 16] for i in range(4)]
    low = jnp.where(c == 0, pieces[0], pieces[2])
    high = jnp.where(c == 0, pieces[1], pieces[3])
    bag[f] = jnp.concatenate([low, high], axis=1).astype(BF16)

    pl.semaphore_wait(barrier, 25)

    for b in FAR + (0,):
        for s in (1, 0):
            if (b, s) != (0, 0):
                remote(bag.at[f], bag.at[f], ag_send, ag_recv.at[b], plane(0, b, s)).start()
    remote(tok_in, tok.at[mine], core_send.at[0], core_recv, other).start()
    for q in (0, 3, 1, 2):
        cols = pl.ds(pl.multiple_of((2 * q + oc) * SPAN, 128), SPAN)
        remote(og_in.at[:, cols], og.at[q, mine], core_send.at[1], og_recv.at[q], other).start()
    for b in (0, 1, 7, 2, 6, 3, 5, 4):
        await_bytes(bag.at[pl.ds(0, 2 if b else 1)], ag_recv.at[b])
        pair = bag.at[pl.ds(16 * x + 2 * ((z + 8 - b) % 8), 2)]
        for o in (2, 1, 3):
            remote(pair, pair, fw_send, fw_recv.at[o - 1], xs[o]).start()

    await_bytes(tok.at[mine], ld_sem.at[0])
    await_bytes(tok.at[mine], core_recv)
    lane = lax.broadcasted_iota(jnp.int32, (16, 128), 1)
    half = None
    for o in (0, 1, 3, 2):
        at = (x + 4 - o) % 4
        if o:
            await_bytes(bag.at[pl.ds(0, 16)], fw_recv.at[o - 1])
        tops, bottoms = [], []
        for k in range(8):
            even = bag[16 * at + 2 * k].astype(F32)
            odd = bag[16 * at + 2 * k + 1].astype(F32)
            tops.append(jnp.where(lane < 64, even, pltpu.roll(odd, 64, axis=1)).astype(BF16))
            bottoms.append(jnp.where(lane < 64, pltpu.roll(even, 64, axis=1), odd).astype(BF16))
        basis_t = jnp.concatenate(
            [jnp.concatenate(tops, axis=1), jnp.concatenate(bottoms, axis=1)], axis=0
        )
        term = lax.dot_general(
            basis_t,
            tok[:, pl.ds(pl.multiple_of(1024 * at, 1024), 1024)],
            (((1,), (1,)), ((), ())),
            preferred_element_type=F32,
        )
        half = term if half is None else half + term
    cot[c] = half.astype(BF16)
    remote(cot.at[c], cot.at[c], cot_send, cot_recv, other).start()
    await_bytes(cot.at[c], cot_recv)
    coords_t = cot[...].reshape(RANK, 2 * TOK)

    await_bytes(og.at[:, mine], ld_sem.at[1])
    for q in (0, 3, 1, 2):
        await_bytes(og.at[q, mine], og_recv.at[q])
        part = jnp.dot(coords_t, og[q], preferred_element_type=F32)
        if q == 3:
            for to in range(8):
                s, start = to // 4, 128 * STARTS[to % 4]
                zs3[to] = jnp.concatenate(
                    [part[16 * i + 8 * s : 16 * i + 8 * s + 8, start : start + WIN] for i in range(4)],
                    axis=0,
                ).astype(BF16)
            for o in FAR:
                to = (z + o) % 8
                remote(
                    zs3.at[to], zr3.at[o - 1], z_send.at[2], z_recv.at[2], dev(x, y, to, c)
                ).start()
        else:
            part = part.astype(BF16)
            for i in range(4):
                g[q, i] = part[16 * i : 16 * i + 16]
            for o in (2, 1, 3):
                remote(
                    g.at[q, (x + o) % 4], xr.at[q, o - 1], x_send.at[q], x_recv.at[q], xs[o]
                ).start()

    for o in FAR:
        signal(ready, dev(x, (y + o) % 8, z, c))

    def along_x(q):
        await_bytes(xr.at[q], x_recv.at[q])
        total = g[q, x].astype(F32)
        for o in range(3):
            total = total + xr[q, o].astype(F32)
        return total

    sums = [along_x(0), along_x(1)]
    for to in range(8):
        s, start = to // 4, 128 * STARTS[to % 4]
        zs[to] = jnp.concatenate(
            [t[8 * s : 8 * s + 8, start : start + WIN] for t in sums], axis=0
        ).astype(BF16)
    for o in FAR:
        to = (z + o) % 8
        remote(zs.at[to], zr.at[o - 1], z_send.at[0], z_recv.at[0], dev(x, y, to, c)).start()

    await_bytes(zr3, z_recv.at[2])
    total = zs3[z].astype(F32)
    for o in range(7):
        total = total + zr3[o].astype(F32)
    for i in range(4):
        xs3[i] = total[8 * i : 8 * i + 8]
    for o in (2, 1, 3):
        remote(xs3.at[(x + o) % 4], xr3.at[o - 1], x_send.at[3], x_recv.at[3], xs[o]).start()

    total = along_x(2)
    for to in range(8):
        s, start = to // 4, 128 * STARTS[to % 4]
        rows = total[8 * s : 8 * s + 8]
        zs2[to] = jnp.concatenate(
            [rows[:, start : start + 256], rows[:, start + 256 : start + 512]], axis=0
        ).astype(BF16)
    for o in FAR:
        to = (z + o) % 8
        remote(zs2.at[to], zr2.at[o - 1], z_send.at[1], z_recv.at[1], dev(x, y, to, c)).start()

    pl.semaphore_wait(ready, 7)

    @pl.when(apart)
    def _():
        remote(first_in, mom.at[0], mom_send.at[0], mom_recv.at[0], swap).start()
        remote(second_in, mom.at[1], mom_send.at[1], mom_recv.at[1], swap).start()

    @pl.when(alone)
    def _():
        pltpu.make_async_copy(first_in, mom.at[0], mom_recv.at[0]).start()
        pltpu.make_async_copy(second_in, mom.at[1], mom_recv.at[1]).start()

    def along_y(total, q):
        total = pltpu.roll(total, 512 - 64 * (z % 2), axis=1)
        blocks = [total[:, :256], pltpu.roll(total, 512 - UNIT, axis=1)[:, :256]]
        for r in range(2):
            to = 2 * q + r
            ys[to] = blocks[r]

            @pl.when(y != to)
            def _():
                slot = (to + 8 - y) % 8 - 1
                remote(ys.at[to], yr.at[slot], y_send, y_recv, dev(x, to, z, c)).start()

    await_bytes(xr3, x_recv.at[3])
    total = xs3[x]
    for o in range(3):
        total = total + xr3[o]
    along_y(total, 3)

    await_bytes(zr, z_recv.at[0])
    total = zs[z].astype(F32)
    for o in range(7):
        total = total + zr[o].astype(F32)
    along_y(total[:8], 0)
    along_y(total[8:], 1)

    await_bytes(zr2, z_recv.at[1])
    total = zs2[z].astype(F32)
    for o in range(7):
        total = total + zr2[o].astype(F32)
    along_y(jnp.concatenate([total[:8], total[8:]], axis=1), 2)

    await_bytes(mom.at[0], mom_recv.at[0])
    await_bytes(mom.at[1], mom_recv.at[1])
    await_bytes(yr, y_recv)
    total = ys[y]
    for o in range(7):
        total = total + yr[o]
    grad = total[:, :UNIT]
    new_first = beta_one * mom[0] + (1.0 - beta_one) * grad
    new_second = beta_two * mom[1] + (1.0 - beta_two) * grad * grad
    new[0] = new_first
    new[1] = new_second

    @pl.when(apart)
    def _():
        remote(new, new_out, new_send, new_recv, swap).start()

    @pl.when(alone)
    def _():
        pltpu.make_async_copy(new, new_out, new_recv).start()

    step = new_first / corr_one / (jnp.sqrt(new_second / corr_two) + adam_eps)
    step = jnp.concatenate([step, jnp.zeros((8, 256 - UNIT), F32)], axis=1)
    step = pltpu.roll(step, (96 * (2 * z + p)) % 128, axis=1)
    tile[...] = jnp.concatenate([step[:, :128], step[:, 128:]], axis=0).astype(BF16)
    offsets = [(a, b, s) for a in range(4) for b in range(8) for s in range(2)][1:]
    offsets.sort(key=lambda o: -(min(o[0], 4 - o[0]) + min(o[1], 8 - o[1]) + o[2]))
    for o in offsets:
        remote(tile, sag.at[f], st_send, st_recv, plane(*o)).start()
    pltpu.make_async_copy(tile, sag.at[f], st_own).start()

    await_bytes(bag.at[pl.ds(0, 15)], ag_send)
    await_bytes(bag.at[pl.ds(0, 48)], fw_send)
    await_bytes(tok.at[mine], core_send.at[0])
    await_bytes(og.at[:, mine], core_send.at[1])
    await_bytes(cot.at[c], cot_send)
    for q in range(3):
        await_bytes(xr.at[q], x_send.at[q])
    await_bytes(xr3, x_send.at[3])
    await_bytes(zr, z_send.at[0])
    await_bytes(zr2, z_send.at[1])
    await_bytes(zr3, z_send.at[2])
    await_bytes(yr, y_send)

    @pl.when(apart)
    def _():
        await_bytes(mom.at[0], mom_send.at[0])
        await_bytes(mom.at[1], mom_send.at[1])
        await_bytes(new, new_send)

    await_bytes(tile, st_own)
    await_bytes(sag.at[pl.ds(0, 63)], st_send)
    await_bytes(sag.at[pl.ds(0, 63)], st_recv)
    await_bytes(new, new_recv)


def finish(basis_in, sag, new_in, upd_out, first_out, second_out, bas, st, upd, sem):
    loads = [pltpu.make_async_copy(basis_in, bas, sem.at[0])]
    for b in range(2):
        at = pl.ds(4 * b, 4)
        loads.append(pltpu.make_async_copy(sag.at[:, at], st.at[:, at], sem.at[1 + b]))
    moves = [
        pltpu.make_async_copy(new_in.at[0], first_out, sem.at[3]),
        pltpu.make_async_copy(new_in.at[1], second_out, sem.at[4]),
    ]
    for copy in loads + moves:
        copy.start()

    row = lax.broadcasted_iota(jnp.int32, (RANK, 128), 0)
    col = lax.broadcasted_iota(jnp.int32, (RANK, 128), 1)
    loads[0].wait()
    left = []
    for s in range(2):
        hit = col == (row // 8) * 16 + row % 8 + 8 * s
        one = jnp.where(hit, -step_rate, 0.0).astype(BF16)
        left.append(jnp.dot(bas[...], one, preferred_element_type=F32).astype(BF16))
    left = jnp.concatenate(left, axis=0)

    for b in range(2):
        loads[1 + b].wait()
        right = jnp.concatenate(
            [jnp.concatenate([st[i, 4 * b + j] for i in range(8)], axis=0) for j in range(4)],
            axis=1,
        )
        both = jnp.dot(left, right, preferred_element_type=F32)
        l = [both[:RANK, 128 * j : 128 * j + 128] for j in range(4)]
        u = [both[RANK:, 128 * j : 128 * j + 128] for j in range(4)]
        tiles = [
            l[0],
            jnp.where(col < 96, u[0], l[1]),
            u[1],
            jnp.where(col < 64, l[1], l[2]),
            u[2],
            jnp.where(col < 32, l[2], l[3]),
            u[3],
        ]
        upd[b] = jnp.concatenate(tiles, axis=1).astype(BF16)
        moves.append(
            pltpu.make_async_copy(
                upd.at[b], upd_out.at[:, pl.ds(896 * b, 896)], sem.at[5 + b]
            )
        )
        moves[-1].start()
    for copy in moves:
        copy.wait()


def per_device(tokens, out_grad, basis, first_moment, second_moment):
    hbm = pl.BlockSpec(memory_space=pltpu.HBM)
    dma = pltpu.SemaphoreType.DMA
    steps, moments = pl.pallas_call(
        kernel,
        out_shape=(
            jax.ShapeDtypeStruct((64, 16, 128), BF16),
            jax.ShapeDtypeStruct((2, 8, UNIT), F32),
        ),
        in_specs=[hbm] * 5,
        out_specs=[hbm] * 2,
        scratch_shapes=[
            pltpu.VMEM((RANK, RANK), BF16),
            pltpu.VMEM((2 * TOK, D), BF16),
            pltpu.VMEM((4, 2 * TOK, SPAN), BF16),
            pltpu.VMEM((64, 16, 128), BF16),
            pltpu.VMEM((2, RANK // 2, 2 * TOK), BF16),
            pltpu.VMEM((3, NX, 16, SPAN), BF16),
            pltpu.VMEM((3, NX - 1, 16, SPAN), BF16),
            pltpu.VMEM((NZ, 16, WIN), BF16),
            pltpu.VMEM((NZ - 1, 16, WIN), BF16),
            pltpu.VMEM((NZ, 16, WIN // 2), BF16),
            pltpu.VMEM((NZ - 1, 16, WIN // 2), BF16),
            pltpu.VMEM((NZ, 32, WIN), BF16),
            pltpu.VMEM((NZ - 1, 32, WIN), BF16),
            pltpu.VMEM((NX, 8, WIN), F32),
            pltpu.VMEM((NX - 1, 8, WIN), F32),
            pltpu.VMEM((NY, 8, 256), F32),
            pltpu.VMEM((NY - 1, 8, 256), F32),
            pltpu.VMEM((16, 128), BF16),
            pltpu.VMEM((2, 8, UNIT), F32),
            pltpu.VMEM((2, 8, UNIT), F32),
            dma((3,)),
            dma((2,)), dma, dma((4,)),
            dma, dma((8,)), dma, dma((3,)),
            dma, dma,
            dma((4,)), dma((4,)),
            dma((3,)), dma((3,)),
            dma, dma,
            dma((2,)), dma((2,)),
            dma, dma,
            dma, dma, dma,
            pltpu.SemaphoreType.REGULAR,
        ],
        compiler_params=pltpu.CompilerParams(
            collective_id=0, has_side_effects=True, vmem_limit_bytes=60 << 20
        ),
    )(tokens, out_grad, basis, first_moment, second_moment)
    return pl.pallas_call(
        finish,
        out_shape=(
            jax.ShapeDtypeStruct((RANK, SPAN), BF16),
            jax.ShapeDtypeStruct((8, UNIT), F32),
            jax.ShapeDtypeStruct((8, UNIT), F32),
        ),
        in_specs=[hbm] * 3,
        out_specs=[hbm] * 3,
        scratch_shapes=[
            pltpu.VMEM((RANK, RANK), BF16),
            pltpu.VMEM((8, 8, 16, 128), BF16),
            pltpu.VMEM((2, RANK, SPAN // 2), BF16),
            dma((7,)),
        ],
        compiler_params=pltpu.CompilerParams(vmem_limit_bytes=60 << 20),
    )(basis, steps.reshape(8, 8, 16, 128), moments)


def solution(mesh):
    placed = (
        P(("dp", "fsdp"), None),
        P(("dp", "fsdp"), None),
        P("fsdp", None),
        P("dp", "fsdp"),
        P("dp", "fsdp"),
    )
    return jax.shard_map(
        per_device,
        mesh=mesh,
        in_specs=placed,
        out_specs=(P("fsdp", "dp"), P("dp", "fsdp"), P("dp", "fsdp")),
        check_vma=False,
    )
```

time: 893 us -> 56.7 us (0.06)
  the two profiles are of different devices: /device:TPU:16 before, /device:TPU:1 now
where the time goes in v2:
time: 56.7 us; the launch traced here: 56.4 us
  Pallas kernels  55.8 us (98%)
  between operations  0.64 us (1%)
    pallas_call x1, Pallas kernels, per_device(): pl.pallas_call(kernel, out_shape=(jax.ShapeDtypeStruct((64, 16, 128), BF1...  53.8 us
    pallas_call x1, Pallas kernels, per_device(): pl.pallas_call(finish, out_shape=(jax.ShapeDtypeStruct((RANK, SPAN), BF16...  1.98 us

profile of v2, /device:TPU:1, one launch (start us, length us, event | category | flops | bytes accessed | tf_op | source)
XLA Modules:
  0.0 56.4 jit_solution(4818259703200740432)
XLA Ops:
  0.6 53.8 %shard_map.76 = (bf16[64,16,128]{2,1,0:T(8,128)(2,1)}, f32[2,8,224]{2,1,0:T(8,128)}) custom-call(bf16[128,4096]{1,0:T(8,128)(2,1)} %tok_in.1, bf16[128,14336]{1,0:T(8,128)(2,1)} %og_in.1, bf16[64,64]{1,0:T(8,128)(2,1)} %basis_in.3, f32[8,224]{1,0:T(8,128)} %first_in.1, f32[8,224]{1,0:T(8,128)} %second_in.1), custom_call_target="tpu_custom_call" | custom-call | tf_op jit(solution)/shard_map/pallas_call | solution.py:355
  54.4 2.0 %shard_map.77 = (bf16[64,1792]{1,0:T(8,128)(2,1)}, f32[8,224]{1,0:T(8,128)}, f32[8,224]{1,0:T(8,128)}) custom-call(bf16[64,64]{1,0:T(8,128)(2,1)} %basis_in.3, bf16[8,8,16,128]{3,2,1,0:T(8,128)(2,1)} %bitcast.1, f32[2,8,224]{2,1,0:T(8,128)} %get-tuple-element.6.new_in), custom_call_target="tpu_custom_call" | custom-call | tf_op jit(solution)/shard_map/pallas_call | solution.py:400

commit v3 on v2

--- a/solution.py
+++ b/solution.py
@@ -31,7 +31,7 @@
 def kernel(
     tok_in, og_in, basis_in, first_in, second_in,
     sag, new_out,
-    bas, tok, og, bag, cot, g, xr, zs, zr, zs2, zr2, zs3, zr3, xs3, xr3, ys, yr, tile, mom, new,
+    bas, tok, og, bag, cot, g, xr, zs, zr, zs3, zr3, xs3, xr3, ys, yr, tile, mom, new,
     ld_sem, core_send, core_recv, og_recv, ag_send, ag_recv, fw_send, fw_recv, cot_send, cot_recv,
     x_send, x_recv, z_send, z_recv, y_send, y_recv, mom_send, mom_recv, new_send, new_recv,
     st_send, st_recv, st_own, ready,
@@ -135,6 +135,9 @@
     await_bytes(cot.at[c], cot_recv)
     coords_t = cot[...].reshape(RANK, 2 * TOK)
 
+    for o in FAR:
+        signal(ready, dev(x, (y + o) % 8, z, c))
+
     await_bytes(og.at[:, mine], ld_sem.at[1])
     for q in (0, 3, 1, 2):
         await_bytes(og.at[q, mine], og_recv.at[q])
@@ -149,7 +152,7 @@
             for o in FAR:
                 to = (z + o) % 8
                 remote(
-                    zs3.at[to], zr3.at[o - 1], z_send.at[2], z_recv.at[2], dev(x, y, to, c)
+                    zs3.at[to], zr3.at[o - 1], z_send.at[3], z_recv.at[3], dev(x, y, to, c)
                 ).start()
         else:
             part = part.astype(BF16)
@@ -160,27 +163,40 @@
                     g.at[q, (x + o) % 4], xr.at[q, o - 1], x_send.at[q], x_recv.at[q], xs[o]
                 ).start()
 
-    for o in FAR:
-        signal(ready, dev(x, (y + o) % 8, z, c))
-
-    def along_x(q):
+    def along_z(q):
         await_bytes(xr.at[q], x_recv.at[q])
         total = g[q, x].astype(F32)
         for o in range(3):
             total = total + xr[q, o].astype(F32)
-        return total
-
-    sums = [along_x(0), along_x(1)]
-    for to in range(8):
-        s, start = to // 4, 128 * STARTS[to % 4]
-        zs[to] = jnp.concatenate(
-            [t[8 * s : 8 * s + 8, start : start + WIN] for t in sums], axis=0
-        ).astype(BF16)
-    for o in FAR:
-        to = (z + o) % 8
-        remote(zs.at[to], zr.at[o - 1], z_send.at[0], z_recv.at[0], dev(x, y, to, c)).start()
-
-    await_bytes(zr3, z_recv.at[2])
+        for to in range(8):
+            s, start = to // 4, 128 * STARTS[to % 4]
+            rows = total[8 * s : 8 * s + 8]
+            zs[q, to] = jnp.concatenate(
+                [rows[:, start : start + 256], rows[:, start + 256 : start + 512]], axis=0
+            ).astype(BF16)
+        for o in FAR:
+            to = (z + o) % 8
+            remote(
+                zs.at[q, to], zr.at[q, o - 1], z_send.at[q], z_recv.at[q], dev(x, y, to, c)
+            ).start()
+
+    along_z(0)
+
+    pl.semaphore_wait(ready, 7)
+
+    @pl.when(apart)
+    def _():
+        remote(first_in, mom.at[0], mom_send.at[0], mom_recv.at[0], swap).start()
+        remote(second_in, mom.at[1], mom_send.at[1], mom_recv.at[1], swap).start()
+
+    @pl.when(alone)
+    def _():
+        pltpu.make_async_copy(first_in, mom.at[0], mom_recv.at[0]).start()
+        pltpu.make_async_copy(second_in, mom.at[1], mom_recv.at[1]).start()
+
+    along_z(1)
+
+    await_bytes(zr3, z_recv.at[3])
     total = zs3[z].astype(F32)
     for o in range(7):
         total = total + zr3[o].astype(F32)
@@ -189,28 +205,7 @@
     for o in (2, 1, 3):
         remote(xs3.at[(x + o) % 4], xr3.at[o - 1], x_send.at[3], x_recv.at[3], xs[o]).start()
 
-    total = along_x(2)
-    for to in range(8):
-        s, start = to // 4, 128 * STARTS[to % 4]
-        rows = total[8 * s : 8 * s + 8]
-        zs2[to] = jnp.concatenate(
-            [rows[:, start : start + 256], rows[:, start + 256 : start + 512]], axis=0
-        ).astype(BF16)
-    for o in FAR:
-        to = (z + o) % 8
-        remote(zs2.at[to], zr2.at[o - 1], z_send.at[1], z_recv.at[1], dev(x, y, to, c)).start()
-
-    pl.semaphore_wait(ready, 7)
-
-    @pl.when(apart)
-    def _():
-        remote(first_in, mom.at[0], mom_send.at[0], mom_recv.at[0], swap).start()
-        remote(second_in, mom.at[1], mom_send.at[1], mom_recv.at[1], swap).start()
-
-    @pl.when(alone)
-    def _():
-        pltpu.make_async_copy(first_in, mom.at[0], mom_recv.at[0]).start()
-        pltpu.make_async_copy(second_in, mom.at[1], mom_recv.at[1]).start()
+    along_z(2)
 
     def along_y(total, q):
         total = pltpu.roll(total, 512 - 64 * (z % 2), axis=1)
@@ -224,24 +219,22 @@
                 slot = (to + 8 - y) % 8 - 1
                 remote(ys.at[to], yr.at[slot], y_send, y_recv, dev(x, to, z, c)).start()
 
+    def end_z(q):
+        await_bytes(zr.at[q], z_recv.at[q])
+        total = zs[q, z].astype(F32)
+        for o in range(7):
+            total = total + zr[q, o].astype(F32)
+        along_y(jnp.concatenate([total[:8], total[8:]], axis=1), q)
+
+    end_z(0)
+    end_z(1)
     await_bytes(xr3, x_recv.at[3])
     total = xs3[x]
     for o in range(3):
         total = total + xr3[o]
     along_y(total, 3)
 
-    await_bytes(zr, z_recv.at[0])
-    total = zs[z].astype(F32)
-    for o in range(7):
-        total = total + zr[o].astype(F32)
-    along_y(total[:8], 0)
-    along_y(total[8:], 1)
-
-    await_bytes(zr2, z_recv.at[1])
-    total = zs2[z].astype(F32)
-    for o in range(7):
-        total = total + zr2[o].astype(F32)
-    along_y(jnp.concatenate([total[:8], total[8:]], axis=1), 2)
+    end_z(2)
 
     await_bytes(mom.at[0], mom_recv.at[0])
     await_bytes(mom.at[1], mom_recv.at[1])
@@ -280,10 +273,9 @@
     await_bytes(cot.at[c], cot_send)
     for q in range(3):
         await_bytes(xr.at[q], x_send.at[q])
+        await_bytes(zr.at[q], z_send.at[q])
+    await_bytes(zr3, z_send.at[3])
     await_bytes(xr3, x_send.at[3])
-    await_bytes(zr, z_send.at[0])
-    await_bytes(zr2, z_send.at[1])
-    await_bytes(zr3, z_send.at[2])
     await_bytes(yr, y_send)
 
     @pl.when(apart)
@@ -368,10 +360,8 @@
             pltpu.VMEM((2, RANK // 2, 2 * TOK), BF16),
             pltpu.VMEM((3, NX, 16, SPAN), BF16),
             pltpu.VMEM((3, NX - 1, 16, SPAN), BF16),
-            pltpu.VMEM((NZ, 16, WIN), BF16),
-            pltpu.VMEM((NZ - 1, 16, WIN), BF16),
-            pltpu.VMEM((NZ, 16, WIN // 2), BF16),
-            pltpu.VMEM((NZ - 1, 16, WIN // 2), BF16),
+            pltpu.VMEM((3, NZ, 16, WIN // 2), BF16),
+            pltpu.VMEM((3, NZ - 1, 16, WIN // 2), BF16),
             pltpu.VMEM((NZ, 32, WIN), BF16),
             pltpu.VMEM((NZ - 1, 32, WIN), BF16),
             pltpu.VMEM((NX, 8, WIN), F32),
@@ -386,7 +376,7 @@
             dma, dma((8,)), dma, dma((3,)),
             dma, dma,
             dma((4,)), dma((4,)),
-            dma((3,)), dma((3,)),
+            dma((4,)), dma((4,)),
             dma, dma,
             dma((2,)), dma((2,)),
             dma, dma,

time: 56.7 us -> 55.4 us (0.977)
  the two profiles are of different devices: /device:TPU:1 before, /device:TPU:5 now
where the time goes in v3:
time: 55.4 us; the launch traced here: 55.1 us
  Pallas kernels  54.5 us (98%)
  between operations  0.64 us (1%)
    pallas_call x1, Pallas kernels, per_device(): pl.pallas_call(kernel, out_shape=(jax.ShapeDtypeStruct((64, 16, 128), BF1...  52.5 us
    pallas_call x1, Pallas kernels, per_device(): pl.pallas_call(finish, out_shape=(jax.ShapeDtypeStruct((RANK, SPAN), BF16...  1.98 us

profile of v3, /device:TPU:5, one launch (start us, length us, event | category | flops | bytes accessed | tf_op | source)
XLA Modules:
  0.0 55.1 jit_solution(1171891467366870795)
XLA Ops:
  0.6 52.5 %shard_map.76 = (bf16[64,16,128]{2,1,0:T(8,128)(2,1)}, f32[2,8,224]{2,1,0:T(8,128)}) custom-call(bf16[128,4096]{1,0:T(8,128)(2,1)} %tok_in.1, bf16[128,14336]{1,0:T(8,128)(2,1)} %og_in.1, bf16[64,64]{1,0:T(8,128)(2,1)} %basis_in.3, f32[8,224]{1,0:T(8,128)} %first_in.1, f32[8,224]{1,0:T(8,128)} %second_in.1), custom_call_target="tpu_custom_call" | custom-call | tf_op jit(solution)/shard_map/pallas_call | solution.py:347
  53.2 2.0 %shard_map.77 = (bf16[64,1792]{1,0:T(8,128)(2,1)}, f32[8,224]{1,0:T(8,128)}, f32[8,224]{1,0:T(8,128)}) custom-call(bf16[64,64]{1,0:T(8,128)(2,1)} %basis_in.3, bf16[8,8,16,128]{3,2,1,0:T(8,128)(2,1)} %bitcast.1, f32[2,8,224]{2,1,0:T(8,128)} %get-tuple-element.6.new_in), custom_call_target="tpu_custom_call" | custom-call | tf_op jit(solution)/shard_map/pallas_call | solution.py:390

commit v4 on v3

--- a/solution.py
+++ b/solution.py
@@ -46,9 +46,10 @@
     def dev(x_, y_, z_, c_):
         return ((y_ // 2) * 2 + c_, (x_ * 8 + z_) * 2 + y_ % 2)
 
-    swap = dev(h, 2 * x + p, 4 * c + z % 4, z // 4)
-    alone = jnp.logical_and(x == h, z // 4 == c)
-    apart = jnp.logical_not(alone)
+    rx, kz = (x + 2) % 4, (z + 2) % 4
+    owner = dev(h, 2 * rx + p, 4 * c + kz, z // 4)
+    taker = dev((h + 2) % 4, 2 * x + p, 4 * c + kz, z // 4)
+    role = 16 * rx + 8 * (z // 4) + 2 * kz + p
     other = dev(x, y, z, oc)
     xs = [dev((x + o) % 4, y, z, c) for o in range(4)]
 
@@ -144,7 +145,7 @@
         part = jnp.dot(coords_t, og[q], preferred_element_type=F32)
         if q == 3:
             for to in range(8):
-                s, start = to // 4, 128 * STARTS[to % 4]
+                s, start = to // 4, 128 * STARTS[(to + 2) % 4]
                 zs3[to] = jnp.concatenate(
                     [part[16 * i + 8 * s : 16 * i + 8 * s + 8, start : start + WIN] for i in range(4)],
                     axis=0,
@@ -160,16 +161,16 @@
                 g[q, i] = part[16 * i : 16 * i + 16]
             for o in (2, 1, 3):
                 remote(
-                    g.at[q, (x + o) % 4], xr.at[q, o - 1], x_send.at[q], x_recv.at[q], xs[o]
+                    g.at[q, (rx + o) % 4], xr.at[q, o - 1], x_send.at[q], x_recv.at[q], xs[o]
                 ).start()
 
     def along_z(q):
         await_bytes(xr.at[q], x_recv.at[q])
-        total = g[q, x].astype(F32)
+        total = g[q, rx].astype(F32)
         for o in range(3):
             total = total + xr[q, o].astype(F32)
         for to in range(8):
-            s, start = to // 4, 128 * STARTS[to % 4]
+            s, start = to // 4, 128 * STARTS[(to + 2) % 4]
             rows = total[8 * s : 8 * s + 8]
             zs[q, to] = jnp.concatenate(
                 [rows[:, start : start + 256], rows[:, start + 256 : start + 512]], axis=0
@@ -184,15 +185,8 @@
 
     pl.semaphore_wait(ready, 7)
 
-    @pl.when(apart)
-    def _():
-        remote(first_in, mom.at[0], mom_send.at[0], mom_recv.at[0], swap).start()
-        remote(second_in, mom.at[1], mom_send.at[1], mom_recv.at[1], swap).start()
-
-    @pl.when(alone)
-    def _():
-        pltpu.make_async_copy(first_in, mom.at[0], mom_recv.at[0]).start()
-        pltpu.make_async_copy(second_in, mom.at[1], mom_recv.at[1]).start()
+    remote(first_in, mom.at[0], mom_send.at[0], mom_recv.at[0], taker).start()
+    remote(second_in, mom.at[1], mom_send.at[1], mom_recv.at[1], taker).start()
 
     along_z(1)
 
@@ -203,7 +197,7 @@
     for i in range(4):
         xs3[i] = total[8 * i : 8 * i + 8]
     for o in (2, 1, 3):
-        remote(xs3.at[(x + o) % 4], xr3.at[o - 1], x_send.at[3], x_recv.at[3], xs[o]).start()
+        remote(xs3.at[(rx + o) % 4], xr3.at[o - 1], x_send.at[3], x_recv.at[3], xs[o]).start()
 
     along_z(2)
 
@@ -229,7 +223,7 @@
     end_z(0)
     end_z(1)
     await_bytes(xr3, x_recv.at[3])
-    total = xs3[x]
+    total = xs3[rx]
     for o in range(3):
         total = total + xr3[o]
     along_y(total, 3)
@@ -248,13 +242,7 @@
     new[0] = new_first
     new[1] = new_second
 
-    @pl.when(apart)
-    def _():
-        remote(new, new_out, new_send, new_recv, swap).start()
-
-    @pl.when(alone)
-    def _():
-        pltpu.make_async_copy(new, new_out, new_recv).start()
+    remote(new, new_out, new_send, new_recv, owner).start()
 
     step = new_first / corr_one / (jnp.sqrt(new_second / corr_two) + adam_eps)
     step = jnp.concatenate([step, jnp.zeros((8, 256 - UNIT), F32)], axis=1)
@@ -263,8 +251,8 @@
     offsets = [(a, b, s) for a in range(4) for b in range(8) for s in range(2)][1:]
     offsets.sort(key=lambda o: -(min(o[0], 4 - o[0]) + min(o[1], 8 - o[1]) + o[2]))
     for o in offsets:
-        remote(tile, sag.at[f], st_send, st_recv, plane(*o)).start()
-    pltpu.make_async_copy(tile, sag.at[f], st_own).start()
+        remote(tile, sag.at[role], st_send, st_recv, plane(*o)).start()
+    pltpu.make_async_copy(tile, sag.at[role], st_own).start()
 
     await_bytes(bag.at[pl.ds(0, 15)], ag_send)
     await_bytes(bag.at[pl.ds(0, 48)], fw_send)
@@ -278,12 +266,9 @@
     await_bytes(xr3, x_send.at[3])
     await_bytes(yr, y_send)
 
-    @pl.when(apart)
-    def _():
-        await_bytes(mom.at[0], mom_send.at[0])
-        await_bytes(mom.at[1], mom_send.at[1])
-        await_bytes(new, new_send)
-
+    await_bytes(mom.at[0], mom_send.at[0])
+    await_bytes(mom.at[1], mom_send.at[1])
+    await_bytes(new, new_send)
     await_bytes(tile, st_own)
     await_bytes(sag.at[pl.ds(0, 63)], st_send)
     await_bytes(sag.at[pl.ds(0, 63)], st_recv)

time: 55.4 us -> 54.8 us (0.989)
  the two profiles are of different devices: /device:TPU:5 before, /device:TPU:1 now
where the time goes in v4:
time: 54.8 us; the launch traced here: 54.5 us
  Pallas kernels  53.9 us (98%)
  between operations  0.64 us (1%)
    pallas_call x1, Pallas kernels, per_device(): pl.pallas_call(kernel, out_shape=(jax.ShapeDtypeStruct((64, 16, 128), BF1...  51.9 us
    pallas_call x1, Pallas kernels, per_device(): pl.pallas_call(finish, out_shape=(jax.ShapeDtypeStruct((RANK, SPAN), BF16...  1.98 us

profile of v4, /device:TPU:1, one launch (start us, length us, event | category | flops | bytes accessed | tf_op | source)
XLA Modules:
  0.0 54.5 jit_solution(3738373699756963907)
XLA Ops:
  0.6 51.9 %shard_map.76 = (bf16[64,16,128]{2,1,0:T(8,128)(2,1)}, f32[2,8,224]{2,1,0:T(8,128)}) custom-call(bf16[128,4096]{1,0:T(8,128)(2,1)} %tok_in.1, bf16[128,14336]{1,0:T(8,128)(2,1)} %og_in.1, bf16[64,64]{1,0:T(8,128)(2,1)} %basis_in.3, f32[8,224]{1,0:T(8,128)} %first_in.1, f32[8,224]{1,0:T(8,128)} %second_in.1), custom_call_target="tpu_custom_call" | custom-call | tf_op jit(solution)/shard_map/pallas_call | solution.py:332
  52.5 2.0 %shard_map.77 = (bf16[64,1792]{1,0:T(8,128)(2,1)}, f32[8,224]{1,0:T(8,128)}, f32[8,224]{1,0:T(8,128)}) custom-call(bf16[64,64]{1,0:T(8,128)(2,1)} %basis_in.3, bf16[8,8,16,128]{3,2,1,0:T(8,128)(2,1)} %bitcast.1, f32[2,8,224]{2,1,0:T(8,128)} %get-tuple-element.6.new_in), custom_call_target="tpu_custom_call" | custom-call | tf_op jit(solution)/shard_map/pallas_call | solution.py:375
